TPU v7x, 256 devices: a whole 4x4x8 slice. The times are simulated.
256 devices in a mesh: tile: 128 (over z, x, y_hi, core), group: 2 (over y_lo).
Axes of the slice: x: 4, y: 4 (y_hi: 2, y_lo: 2; y = y_hi * 2 + y_lo), z: 8, core: 2. Of those that a mesh axis runs over, the one named last changes fastest.
Arguments:
- state: float32 [8, 5, 128, 128, 128], P('group', None, 'tile'), may hold values from -6 to 6
- courant_x: float32 [8], P('group'), may hold values from -0.35 to 0.35
- courant_y: float32 [8], P('group'), may hold values from -0.35 to 0.35
- diffusion: float32 [5], replicated, may hold values from 0.02 to 0.07
- neighbours: int32 [9, 128, 128, 128], P(None, 'tile'), may hold values from 0 to 16899, as said below
- w_in: bfloat16 [360, 256], replicated, may hold values from -0.3125 to 0.3125
- w_mid: bfloat16 [256, 256], replicated, may hold values from -0.375 to 0.375
- w_out: bfloat16 [256, 40], replicated, may hold values from -0.375 to 0.375
Outputs:
- updated: float32 [8, 5, 128, 128, 128], P('group', None, 'tile')
Inputs may be any that keep to these rules, and one draw needn't show every extreme that they name: `neighbours`: for each column the nine entries name the cells of its 3 x 3 neighbourhood, each once, in one of eight rotated or mirrored orders; cells are numbered in the tile extended by one cell on every side, row by row with 130 cells a row.
All inputs are finite; a program needn't handle non-finite values.
Results may differ from a plain program's by a relative error of at most 0.0016.
Values may be sent and summed in bfloat16 or wider, within the bound.
A program may use at most 128 MiB of HBM per device.

v0:
```python
import jax
import jax.numpy as jnp
import numpy as np
from jax import lax
from jax.experimental import pallas as pl
from jax.experimental.pallas import tpu as pltpu
from jax.sharding import PartitionSpec as P

MESH = pl.DeviceIdType.MESH
F32, BF16 = jnp.float32, jnp.bfloat16
TILE_ROWS = 8
CH = 20
STRIPS = 4
PACK = STRIPS * CH
SLOTS = 18
SENDS = SLOTS // 2
STEPS = 8
KIN = 9 * 48


def feature_rows():
    table = np.full((2, STRIPS, 1, KIN), -1, np.int32)
    lead = {0: (0, 0, 16), 1: (-4, 4, 16), 2: (8, 0, 12), 3: (4, 0, 16)}
    rest = {0: (16, 0, 4), 1: (12, 0, 8), 2: (-8, 8, 16), 3: (-12, 12, 16)}
    for share in range(2):
        for strip in range(STRIPS):
            for slot, owner, (add, low, high) in (
                (0, share, lead[strip]),
                (1, 1 - share, lead[3 - strip]),
                (2, share, rest[strip]),
                (2, 1 - share, rest[3 - strip]),
            ):
                for s in range(low, high):
                    for k in range(9):
                        table[share, strip, 0, 48 * k + 16 * slot + s] = (CH * owner + s + add) * 9 + k
    return table


def kernel(
    state, speed_x, speed_y, spread, near, w_in, w_mid, w_out, table, out,
    xv, s0, s1, coef, edge, from_west, from_east, side, strips, moved_own, moved_sent, packs, arrived,
    z_own, z_sent, z_packs, z_arrived, shifted, masks, xs, ys, v_in, v_mid, v_out, w1, w2, w3, nb, tv,
    t_send, t_arrived, result,
    load_sem, pack_send, pack_recv, z_sem, t_ssem, t_rsem, halo_send, halo_recv, out_sem,
):
    tile = lax.axis_index("tile")
    g = lax.axis_index("group")
    tiles = lax.axis_size("tile")
    ty = lax.rem(tile, TILE_ROWS)
    west = (lax.rem(tile + tiles - 1, tiles), g)
    east = (lax.rem(tile + 1, tiles), g)
    north = (lax.rem(tile + tiles - TILE_ROWS, tiles), g)
    south = (lax.rem(tile + TILE_ROWS, tiles), g)
    partner = (tile, 1 - g)
    own, sent = g, 1 - g
    d_own, d_sent = 2 * own - 1, 2 * sent - 1

    def remote(src, dst, send_sem, recv_sem, device):
        return pltpu.make_async_remote_copy(
            src_ref=src, dst_ref=dst, send_sem=send_sem, recv_sem=recv_sem, device_id=device, device_id_type=MESH
        )

    loads = [
        pltpu.make_async_copy(state, xv, load_sem.at[0]),
        pltpu.make_async_copy(w_in, v_in, load_sem.at[1]),
        pltpu.make_async_copy(w_mid, v_mid, load_sem.at[2]),
        pltpu.make_async_copy(w_out, v_out, load_sem.at[3]),
        pltpu.make_async_copy(
            near.at[0:2, pl.ds(pl.multiple_of(64 * g, 64), 64)], nb, load_sem.at[4]
        ),
        pltpu.make_async_copy(table.at[g], tv, load_sem.at[5]),
    ]
    for load in loads:
        load.start()
    barrier = pltpu.get_barrier_semaphore()
    for device in (west, east, north, south, partner):
        pl.semaphore_signal(barrier, inc=1, device_id=device, device_id_type=MESH)

    chan = lax.broadcasted_iota(jnp.int32, (CH, 128), 0)
    ax = jnp.zeros((CH, 128), F32)
    ay = jnp.zeros((CH, 128), F32)
    nu = jnp.zeros((CH, 128), F32)
    for level in range(4):
        ax = jnp.where(chan // 5 == level, speed_x[level], ax)
        ay = jnp.where(chan // 5 == level, speed_y[level], ay)
    for field in range(5):
        nu = jnp.where(chan % 5 == field, spread[field], nu)
    px, mx = jnp.maximum(ax, 0.0), jnp.minimum(ax, 0.0)
    py, my = jnp.maximum(ay, 0.0), jnp.minimum(ay, 0.0)
    coef[0] = 1.0 - px + mx - py + my - 4.0 * nu
    coef[1] = px + nu
    coef[2] = nu - mx
    coef[3] = py + nu
    coef[4] = nu - my

    lane = lax.broadcasted_iota(jnp.int32, (CH, 128), 1)
    cell = lane % 8

    def substep(center, up, down, left, right):
        return center * coef[0] + up * coef[1] + down * coef[2] + left * coef[3] + right * coef[4]

    def advance_row(src, index):
        center = src[index]
        return substep(
            center, src[index - 1], src[index + 1], pltpu.roll(center, 1, 1), pltpu.roll(center, 127, 1)
        )

    loads[0].wait()
    flat = xv.reshape(CH * 128, 128)

    def spread_rows(i, edges):
        found = []
        for strip in range(8):
            row = flat[pl.ds(16 * strip + i, CH, stride=128), :]
            s0[3 + 16 * strip + i] = row
            found.append(jnp.where(lane // 8 == i, pltpu.roll(row, 8 * i + 4, 1), edges[strip]))
        return tuple(found)

    edges = lax.fori_loop(0, 16, spread_rows, tuple(jnp.zeros((CH, 128), F32) for _ in range(8)))
    for strip in range(8):
        edge[strip] = edges[strip]
    pl.semaphore_wait(barrier, 5)
    to_east = remote(edge, from_west, halo_send.at[0], halo_recv.at[0], east)
    to_west = remote(edge, from_east, halo_send.at[1], halo_recv.at[1], west)
    to_south = remote(s0.at[pl.ds(128, 3)], s0.at[pl.ds(0, 3)], halo_send.at[2], halo_recv.at[2], south)
    to_north = remote(s0.at[pl.ds(3, 3)], s0.at[pl.ds(131, 3)], halo_send.at[3], halo_recv.at[3], north)
    to_east.start()
    to_west.start()
    to_south.start()
    to_north.start()

    def first_rows(start):
        def body(n, carry):
            for u in range(5):
                index = start + 5 * n + u
                s1[index] = advance_row(s0, index)
            return carry

        lax.fori_loop(0, 13, body, 0)

    def pack_of(half, slot, order):
        place = 15 * (1 - half) + (2 * half - 1) * (slot - 1)
        return jnp.concatenate(
            [advance_row(s1, 3 + 64 * half + 16 * strip + place) for strip in order], axis=0
        )

    def pack_copy(s):
        return remote(
            packs.at[pl.ds(2 * s, 2)], arrived.at[pl.ds(2 * s, 2)], pack_send.at[s], pack_recv.at[s], partner
        )

    def send_packs(s, carry):
        for u in range(2):
            value = pack_of(sent, 2 * s + u, (3, 2, 1, 0))
            moved_sent[2 * s + u] = value
            packs[2 * s + u] = value.astype(BF16)
        pack_copy(s).start()
        return carry

    def keep_packs(s, carry):
        for u in range(2):
            moved_own[2 * s + u] = pack_of(own, 2 * s + u, (0, 1, 2, 3))
        return carry

    first_rows(3 + 1 + 61 * sent)
    lax.fori_loop(0, 7, send_packs, 0)

    out_west = cell < jnp.where(ty == 0, 4, 0)
    out_east = cell >= jnp.where(ty == TILE_ROWS - 1, 4, 8)
    to_east.wait()
    to_west.wait()
    for strip in range(8):
        here = edge[strip]
        side[strip + 1, 0] = jnp.where(out_west, 0.0, jnp.where(cell < 4, from_west[strip], here))
        side[strip + 1, 1] = jnp.where(out_east, 0.0, jnp.where(cell < 4, here, from_east[strip]))
    side_south = remote(side.at[8], side.at[0], halo_send.at[4], halo_recv.at[4], south)
    side_north = remote(side.at[1], side.at[9], halo_send.at[5], halo_recv.at[5], north)
    side_south.start()
    side_north.start()

    first_rows(3 + 1 + 61 * own)
    lax.fori_loop(0, 7, keep_packs, 0)

    for load in loads[1:]:
        load.wait()
    source = lax.broadcasted_iota(jnp.int32, (360, KIN), 0)
    for strip in range(STRIPS):
        pick = jnp.where(source == tv[strip], 0.5, 0.0).astype(BF16)
        w1[strip] = lax.dot_general(
            v_in[...], pick, (((0,), (0,)), ((), ())), preferred_element_type=F32
        ).astype(BF16)
    eye = jnp.where(
        lax.broadcasted_iota(jnp.int32, (256, 256), 0) == lax.broadcasted_iota(jnp.int32, (256, 256), 1), 0.5, 0.0
    ).astype(BF16)
    w2[...] = lax.dot_general(
        v_mid[...], eye, (((0,), (0,)), ((), ())), preferred_element_type=F32
    ).astype(BF16)
    place_out = lax.broadcasted_iota(jnp.int32, (PACK, 40), 0)
    chan_out = lax.broadcasted_iota(jnp.int32, (PACK, 40), 1)
    for strip in range(STRIPS):
        for part, at, owner in ((0, strip, g), (1, 3 - strip, 1 - g)):
            c = place_out - CH * at
            pick = jnp.where(
                (c >= 0) & (c < CH) & (chan_out == c + CH * owner), 1.0, 0.0
            ).astype(BF16)
            w3[PACK * part : PACK * (part + 1), 256 * strip : 256 * (strip + 1)] = lax.dot_general(
                pick, v_out[...], (((1,), (1,)), ((), ())), preferred_element_type=F32
            ).astype(BF16)

    to_south.wait()
    to_north.wait()
    for index in (1, 2, 3, 130, 131, 132):
        s1[index] = advance_row(s0, index)
    lax.fori_loop(7, 9, send_packs, 0)

    side_south.wait()
    side_north.wait()
    now = [[side[n, which] for n in range(10)] for which in range(2)]
    for sweep in range(2):
        later = []
        for which in range(2):
            cur = now[which]
            down8 = [pltpu.roll(v, 8, 1) for v in cur]
            up8 = [pltpu.roll(v, 120, 1) for v in cur]
            new = []
            for n in range(10):
                upper = jnp.where(lane < 8, down8[max(n - 1, 0)], down8[n])
                lower = jnp.where(lane >= 120, up8[min(n + 1, 9)], up8[n])
                value = substep(cur[n], upper, lower, pltpu.roll(cur[n], 1, 1), pltpu.roll(cur[n], 127, 1))
                new.append(jnp.where(out_east if which else out_west, 0.0, value))
            later.append(new)
        now = later
    for n in range(10):
        w, e = now[0][n], now[1][n]
        strips[n] = jnp.where(
            cell < 4, e, jnp.where(cell < 6, w, jnp.where(cell == 6, pltpu.roll(e, 2, 1), pltpu.roll(w, 4, 1)))
        )
    for k in range(3):
        at = 4 * sent + 1 + (k - 1) * d_sent
        value = jnp.concatenate([strips[at + q] for q in (3, 2, 1, 0)], axis=0)
        z_sent[k] = value
        z_packs[k] = value.astype(BF16)
    z_copy = remote(z_packs, z_arrived, z_sem.at[0], z_sem.at[1], partner)
    z_copy.start()
    for k in range(3):
        at = 4 * own + 1 + (k - 1) * d_own
        z_own[k] = jnp.concatenate([strips[at + q] for q in range(4)], axis=0)
    lax.fori_loop(7, 9, keep_packs, 0)

    lane1 = lax.broadcasted_iota(jnp.int32, (1, 128), 1)

    def order_masks(m, carry):
        place = 15 * (1 - own) + d_own * m
        flips = [[], [], []]
        for q in range(STRIPS):
            row = 16 * q + place
            centre = (64 * g + row + 1) * 130 + lane1 + 1
            first = nb[0, pl.ds(row, 1), :] - centre
            second = nb[1, pl.ds(row, 1), :] - centre
            flips[0].append(jnp.where(first > 0, 1.0, 0.0))
            flips[1].append(jnp.where((first == -129) | (first == 131), 1.0, 0.0))
            flips[2].append(jnp.where(second * second == 1, 1.0, 0.0))
        for kind in range(3):
            wide = [jnp.broadcast_to(v, (CH, 128)) for v in flips[kind]]
            masks[0, m, kind] = jnp.concatenate(wide, axis=0).astype(BF16)
            masks[1, m, kind] = jnp.concatenate(wide[::-1], axis=0).astype(BF16)
        return carry

    lax.fori_loop(0, 16, order_masks, 0)

    wide_lane = lax.broadcasted_iota(jnp.int32, (PACK, 128), 1)

    def fix_edges(value, z, place):
        return jnp.where((wide_lane < 2) | (wide_lane >= 126), pltpu.roll(z, 124 - 8 * place, 1), value)

    def ingest(slot):
        place = lax.rem(15 * (1 - own) + d_own * (slot - 1) + 16, 16)
        zi = (slot + 16) // 17 + slot // 17
        for which in range(2):
            if which == 0:
                value, z = moved_own[slot], z_own[zi]
            else:
                value, z = arrived[slot].astype(F32), z_arrived[zi].astype(F32)
            value = fix_edges(value, z, place)
            if which == 0:
                moved_own[slot] = value
            ends = pltpu.roll(z, 121 - 8 * place, 1)
            shifted[which, slot, 0] = jnp.where(wide_lane == 0, ends, pltpu.roll(value, 1, 1)).astype(BF16)
            shifted[which, slot, 1] = value.astype(BF16)
            shifted[which, slot, 2] = jnp.where(wide_lane == 127, ends, pltpu.roll(value, 127, 1)).astype(BF16)

    sub = lax.broadcasted_iota(jnp.int32, (16, 128), 0)

    def pick_neighbours(slot, u):
        cols = slice(128 * u, 128 * (u + 1))
        tails = {}
        for which in range(2):
            for t in range(5):
                rows = slice(16 * t, 16 * (t + 1))
                flip_a, flip_b, turn = (masks[which, slot - 1, kind, rows, :] > 0.5 for kind in range(3))
                a = [[shifted[which, slot + d_own * da, b, rows, :] for b in range(3)] for da in (-1, 0, 1)]
                a = [
                    [jnp.where(flip_a, a[2][b], a[0][b]) for b in range(3)],
                    a[1],
                    [jnp.where(flip_a, a[0][b], a[2][b]) for b in range(3)],
                ]
                a = [[jnp.where(flip_b, r[2], r[0]), r[1], jnp.where(flip_b, r[0], r[2])] for r in a]
                for i in range(3):
                    for j in range(3):
                        k = 3 * i + j
                        value = a[i][j] if i == j else jnp.where(turn, a[j][i], a[i][j])
                        strip = {0: 0, 1: 1, 3: 2, 4: 3}.get(t)
                        if strip is not None:
                            q = strip if which == 0 else 3 - strip
                            xs[q, 48 * k + 16 * which : 48 * k + 16 * which + 16, cols] = value
                        if t in (1, 2, 3):
                            tails[which, t, k] = value
        for k in range(9):
            at = slice(48 * k + 32, 48 * k + 48)
            low = sub < 8
            xs[0, at, cols] = jnp.where(low, tails[0, 1, k], tails[1, 3, k])
            xs[1, at, cols] = jnp.where(low, tails[0, 2, k], tails[1, 2, k])
            xs[2, at, cols] = jnp.where(low, tails[1, 2, k], tails[0, 2, k])
            xs[3, at, cols] = jnp.where(low, tails[1, 1, k], tails[0, 3, k])

    def silu_of_double(h):
        return h + h * jnp.tanh(h)

    def store_rows(value, half, place, order):
        for p, q in enumerate(order):
            flat_out[pl.ds(64 * half + 16 * q + place, CH, stride=128), :] = value[CH * p : CH * (p + 1)]

    flat_out = result.reshape(CH * 128, 128)

    def t_copy(t):
        return remote(t_send.at[t], t_arrived.at[t], t_ssem.at[t], t_rsem.at[t], partner)

    z_copy.wait()
    pack_copy(0).wait_recv()
    ingest(0)
    ingest(1)

    def physics(t, carry):
        pack_copy(t + 1).wait_recv()
        ingest(2 * t + 2)
        ingest(2 * t + 3)
        for u in range(2):
            pick_neighbours(2 * t + 1 + u, u)
        for q in range(STRIPS):
            first = silu_of_double(jnp.dot(w1[q], xs[q], preferred_element_type=F32)).astype(BF16)
            second = silu_of_double(jnp.dot(w2[...], first, preferred_element_type=F32)).astype(BF16)
            ys[256 * q : 256 * (q + 1), :] = second
        tendency = jnp.dot(w3[...], ys[...], preferred_element_type=F32).astype(BF16)
        for u in range(2):
            t_send[t, u] = tendency[PACK:, 128 * u : 128 * (u + 1)]
        t_copy(t).start()
        for u in range(2):
            place = 15 * (1 - own) + d_own * (2 * t + u)
            value = moved_own[2 * t + 1 + u] + tendency[:PACK, 128 * u : 128 * (u + 1)].astype(F32)
            store_rows(value, own, place, (0, 1, 2, 3))
        return carry

    lax.fori_loop(0, STEPS, physics, 0)

    def finish(t, carry):
        t_copy(t).wait_recv()
        for u in range(2):
            place = 15 * (1 - sent) + d_sent * (2 * t + u)
            value = fix_edges(moved_sent[2 * t + 1 + u], z_sent[1], place) + t_arrived[t, u].astype(F32)
            store_rows(value, sent, place, (3, 2, 1, 0))
        return carry

    lax.fori_loop(0, STEPS, finish, 0)
    store = pltpu.make_async_copy(result, out, out_sem)
    store.start()
    for s in range(SENDS):
        pack_copy(s).wait_send()
    for t in range(STEPS):
        t_copy(t).wait_send()
    store.wait()


def shards(state, courant_x, courant_y, diffusion, neighbours, w_in, w_mid, w_out):
    levels, fields, single, cells_x, cells_y = state.shape
    chans = levels * fields
    anywhere = pl.BlockSpec(memory_space=pl.ANY)
    scalars = pl.BlockSpec(memory_space=pltpu.SMEM)
    vmem = pltpu.VMEM
    dma = pltpu.SemaphoreType.DMA
    updated = pl.pallas_call(
        kernel,
        out_shape=jax.ShapeDtypeStruct((chans, cells_x, cells_y), F32),
        in_specs=[anywhere, scalars, scalars, scalars, anywhere, anywhere, anywhere, anywhere, anywhere],
        out_specs=anywhere,
        scratch_shapes=[
            vmem((CH, 128, 128), F32),
            vmem((134, CH, 128), F32),
            vmem((134, CH, 128), F32),
            vmem((5, CH, 128), F32),
            vmem((8, CH, 128), F32),
            vmem((8, CH, 128), F32),
            vmem((8, CH, 128), F32),
            vmem((10, 2, CH, 128), F32),
            vmem((10, CH, 128), F32),
            vmem((SLOTS, PACK, 128), F32),
            vmem((SLOTS, PACK, 128), F32),
            vmem((SLOTS, PACK, 128), BF16),
            vmem((SLOTS, PACK, 128), BF16),
            vmem((3, PACK, 128), F32),
            vmem((3, PACK, 128), F32),
            vmem((3, PACK, 128), BF16),
            vmem((3, PACK, 128), BF16),
            vmem((2, SLOTS, 3, PACK, 128), BF16),
            vmem((2, 16, 3, PACK, 128), BF16),
            vmem((STRIPS, KIN, 256), BF16),
            vmem((STRIPS * 256, 256), BF16),
            vmem((360, 256), BF16),
            vmem((256, 256), BF16),
            vmem((256, 40), BF16),
            vmem((STRIPS, 256, KIN), BF16),
            vmem((256, 256), BF16),
            vmem((2 * PACK, STRIPS * 256), BF16),
            vmem((2, 64, 128), jnp.int32),
            vmem((STRIPS, 1, KIN), jnp.int32),
            vmem((STEPS, 2, PACK, 128), BF16),
            vmem((STEPS, 2, PACK, 128), BF16),
            vmem((CH, 128, 128), F32),
            dma((6,)),
            dma((SENDS,)),
            dma((SENDS,)),
            dma((2,)),
            dma((STEPS,)),
            dma((STEPS,)),
            dma((6,)),
            dma((6,)),
            dma,
        ],
        compiler_params=pltpu.CompilerParams(
            collective_id=0, has_side_effects=True, vmem_limit_bytes=48 * 1024 * 1024
        ),
    )(
        state.reshape(chans, cells_x, cells_y),
        courant_x,
        courant_y,
        diffusion,
        neighbours.reshape(9, cells_x, cells_y),
        w_in,
        w_mid,
        w_out,
        jnp.asarray(feature_rows()),
    )
    return updated.reshape(levels, fields, single, cells_x, cells_y)


def solution(mesh):
    return jax.shard_map(
        shards,
        mesh=mesh,
        in_specs=(
            P("group", None, "tile", None, None),
            P("group"),
            P("group"),
            P(),
            P(None, "tile", None, None),
            P(),
            P(),
            P(),
        ),
        out_specs=P("group", None, "tile", None, None),
        check_vma=False,
    )
```

profile of v0, /device:TPU:1, one launch (start us, length us, event | category | flops | bytes accessed | tf_op | source)
XLA Modules:
  0.0 53.8 jit_solution(17985336081199512600)
XLA Ops:
  0.0 0.8 %copy.10.w_out = bf16[256,40]{1,0:T(8,128)(2,1)S(1)} copy(bf16[256,40]{0,1:T(8,128)(2,1)} %param.16) | data formatting | bytes 40960 | tf_op args[7]
  0.8 0.0 copy-start
  0.9 1.3 %copy-done = f32[4,5,1,128,128]{4,3,2,1,0:T(8,128)S(1)} copy-done((f32[4,5,1,128,128]{4,3,2,1,0:T(8,128)S(1)}, f32[4,5,1,128,128]{4,3,2,1,0:T(8,128)}, u32[]{:S(2)}) %copy-start) | copy-done | bytes 1310744
  2.2 0.0 copy-start.1
  2.2 1.1 %copy-done.1 = s32[9,1,128,128]{3,2,1,0:T(8,128)S(1)} copy-done((s32[9,1,128,128]{3,2,1,0:T(8,128)S(1)}, s32[9,1,128,128]{3,2,1,0:T(8,128)}, u32[]{:S(2)}) %copy-start.1) | copy-done | bytes 589848
  3.2 0.0 copy-start.2
  3.2 0.9 %copy-done.2 = bf16[360,256]{1,0:T(8,128)(2,1)S(1)} copy-done((bf16[360,256]{1,0:T(8,128)(2,1)S(1)}, bf16[360,256]{1,0:T(8,128)(2,1)}, u32[]{:S(2)}) %copy-start.2) | copy-done | bytes 184344
  4.2 0.0 copy-start.3
  4.2 0.9 %copy-done.3 = bf16[256,256]{1,0:T(8,128)(2,1)S(1)} copy-done((bf16[256,256]{1,0:T(8,128)(2,1)S(1)}, bf16[256,256]{1,0:T(8,128)(2,1)}, u32[]{:S(2)}) %copy-start.3) | copy-done | bytes 131096
  5.1 0.0 copy-start.4
  5.1 0.7 %copy-done.4 = s32[2,4,1,432]{3,2,1,0:T(1,128)S(1)} copy-done((s32[2,4,1,432]{3,2,1,0:T(1,128)S(1)}, s32[2,4,1,432]{3,2,1,0:T(1,128)}, u32[]{:S(2)}) %copy-start.4) | copy-done | bytes 13848
  5.8 0.0 copy-start.5
  5.8 0.7 %copy-done.5 = f32[4]{0:T(128)S(1)} copy-done((f32[4]{0:T(128)S(1)}, f32[4]{0:T(128)}, u32[]{:S(2)}) %copy-start.5) | copy-done | bytes 40
  6.4 0.0 copy-start.6
  6.4 0.7 %copy-done.6 = f32[4]{0:T(128)S(1)} copy-done((f32[4]{0:T(128)S(1)}, f32[4]{0:T(128)}, u32[]{:S(2)}) %copy-start.6) | copy-done | bytes 40
  7.1 0.0 copy-start.7
  7.1 0.7 %copy-done.7 = f32[5]{0:T(128)S(1)} copy-done((f32[5]{0:T(128)S(1)}, f32[5]{0:T(128)}, u32[]{:S(2)}) %copy-start.7) | copy-done | bytes 44
  7.7 45.0 %shard_map.91 = f32[20,128,128]{2,1,0:T(8,128)S(1)} custom-call(f32[20,128,128]{2,1,0:T(8,128)S(1)} %bitcast.6, f32[4]{0:T(128)S(1)} %copy-done.5, f32[4]{0:T(128)S(1)} %copy-done.6, f32[5]{0:T(128)S(1)} %copy-done.7, s32[9,128,128]{2,1,0:T(8,128)S(1)} %bitcast.7, bf16[360,256]{1,0:T(8,128)(2,1)S(1)} %copy-done.2, bf16[256,256]{1,0:T(8,128)(2,1)S(1)} %copy-done.3, ...), custom_call_target="tpu_custom_call" | custom-call | tf_op jit(solution)/shard_map/pallas_call | solution.py:390
  52.7 1.1 %copy.13 = f32[4,5,1,128,128]{4,3,2,1,0:T(8,128)} copy(f32[4,5,1,128,128]{4,3,2,1,0:T(8,128)S(1)} %bitcast.5) | data formatting | bytes 2621440
Async XLA Ops:
  0.8 1.3 %copy-start = (f32[4,5,1,128,128]{4,3,2,1,0:T(8,128)S(1)}, f32[4,5,1,128,128]{4,3,2,1,0:T(8,128)}, u32[]{:S(2)}) copy-start(f32[4,5,1,128,128]{4,3,2,1,0:T(8,128)} %param.9) | copy-start | bytes 3932164
  2.2 1.1 %copy-start.1 = (s32[9,1,128,128]{3,2,1,0:T(8,128)S(1)}, s32[9,1,128,128]{3,2,1,0:T(8,128)}, u32[]{:S(2)}) copy-start(s32[9,1,128,128]{3,2,1,0:T(8,128)} %param.13) | copy-start | bytes 1769476
  3.2 0.9 %copy-start.2 = (bf16[360,256]{1,0:T(8,128)(2,1)S(1)}, bf16[360,256]{1,0:T(8,128)(2,1)}, u32[]{:S(2)}) copy-start(bf16[360,256]{1,0:T(8,128)(2,1)} %w_in.1) | copy-start | bytes 552964
  4.2 0.9 %copy-start.3 = (bf16[256,256]{1,0:T(8,128)(2,1)S(1)}, bf16[256,256]{1,0:T(8,128)(2,1)}, u32[]{:S(2)}) copy-start(bf16[256,256]{1,0:T(8,128)(2,1)} %w_mid.1) | copy-start | bytes 393220
  5.1 0.7 %copy-start.4 = (s32[2,4,1,432]{3,2,1,0:T(1,128)S(1)}, s32[2,4,1,432]{3,2,1,0:T(1,128)}, u32[]{:S(2)}) copy-start(s32[2,4,1,432]{3,2,1,0:T(1,128)} %constant.2.clone.table) | copy-start | bytes 41476
  5.8 0.7 %copy-start.5 = (f32[4]{0:T(128)S(1)}, f32[4]{0:T(128)}, u32[]{:S(2)}) copy-start(f32[4]{0:T(128)} %speed_x.1) | copy-start | bytes 52
  6.4 0.7 %copy-start.6 = (f32[4]{0:T(128)S(1)}, f32[4]{0:T(128)}, u32[]{:S(2)}) copy-start(f32[4]{0:T(128)} %speed_y.1) | copy-start | bytes 52
  7.1 0.7 %copy-start.7 = (f32[5]{0:T(128)S(1)}, f32[5]{0:T(128)}, u32[]{:S(2)}) copy-start(f32[5]{0:T(128)} %spread.1) | copy-start | bytes 64
where the time goes:
time: 54.1 us; the launch traced here: 53.8 us
  Pallas kernels  45 us (83%)
  local copies, waits for them, and re-layouts  8.79 us (16%)
    pallas_call x1, Pallas kernels, shards(): pl.pallas_call(kernel, out_shape=jax.ShapeDtypeStruct((chans, cells_x, ce...  45 us
    unnamed x18, local copies, waits for them, and re-layouts  8.79 us

commit v1 on v0

--- a/solution.py
+++ b/solution.py
@@ -39,9 +39,9 @@
 def kernel(
     state, speed_x, speed_y, spread, near, w_in, w_mid, w_out, table, out,
     xv, s0, s1, coef, edge, from_west, from_east, side, strips, moved_own, moved_sent, packs, arrived,
-    z_own, z_sent, z_packs, z_arrived, shifted, masks, xs, ys, v_in, v_mid, v_out, w1, w2, w3, nb, tv,
-    t_send, t_arrived, result,
-    load_sem, pack_send, pack_recv, z_sem, t_ssem, t_rsem, halo_send, halo_recv, out_sem,
+    z_own, z_sent, z_packs, z_arrived, shifted, masks, xs_even, xs_odd, ys, v_in, v_mid, v_out, w1, w2, w3, nb, tv,
+    t_send, t_arrived,
+    state_sem, load_sem, pack_send, pack_recv, z_ssem, z_rsem, t_ssem, t_rsem, halo_send, halo_recv,
 ):
     tile = lax.axis_index("tile")
     g = lax.axis_index("group")
@@ -61,7 +61,6 @@
         )
 
     loads = [
-        pltpu.make_async_copy(state, xv, load_sem.at[0]),
         pltpu.make_async_copy(w_in, v_in, load_sem.at[1]),
         pltpu.make_async_copy(w_mid, v_mid, load_sem.at[2]),
         pltpu.make_async_copy(w_out, v_out, load_sem.at[3]),
@@ -70,11 +69,25 @@
         ),
         pltpu.make_async_copy(table.at[g], tv, load_sem.at[5]),
     ]
+    def state_load(n):
+        rows = pl.ds(pl.multiple_of(16 * n, 16), 16)
+        return pltpu.make_async_copy(state.at[:, rows], xv.at[:, rows], state_sem.at[n])
+
+    for n in range(8):
+        state_load(n).start()
     for load in loads:
         load.start()
     barrier = pltpu.get_barrier_semaphore()
-    for device in (west, east, north, south, partner):
+    for device in (north, south, partner):
         pl.semaphore_signal(barrier, inc=1, device_id=device, device_id_type=MESH)
+
+    @pl.when(ty > 0)
+    def _():
+        pl.semaphore_signal(barrier, inc=1, device_id=west, device_id_type=MESH)
+
+    @pl.when(ty < TILE_ROWS - 1)
+    def _():
+        pl.semaphore_signal(barrier, inc=1, device_id=east, device_id_type=MESH)
 
     chan = lax.broadcasted_iota(jnp.int32, (CH, 128), 0)
     ax = jnp.zeros((CH, 128), F32)
@@ -105,27 +118,33 @@
             center, src[index - 1], src[index + 1], pltpu.roll(center, 1, 1), pltpu.roll(center, 127, 1)
         )
 
-    loads[0].wait()
     flat = xv.reshape(CH * 128, 128)
 
-    def spread_rows(i, edges):
-        found = []
-        for strip in range(8):
+    def spread_rows(strip, carry):
+        state_load(strip).wait()
+        edges = jnp.zeros((CH, 128), F32)
+        for i in range(16):
             row = flat[pl.ds(16 * strip + i, CH, stride=128), :]
             s0[3 + 16 * strip + i] = row
-            found.append(jnp.where(lane // 8 == i, pltpu.roll(row, 8 * i + 4, 1), edges[strip]))
-        return tuple(found)
-
-    edges = lax.fori_loop(0, 16, spread_rows, tuple(jnp.zeros((CH, 128), F32) for _ in range(8)))
-    for strip in range(8):
-        edge[strip] = edges[strip]
-    pl.semaphore_wait(barrier, 5)
+            edges = jnp.where(lane // 8 == i, pltpu.roll(row, (8 * i + 4) % 128, 1), edges)
+        edge[strip] = edges
+        return carry
+
+    lax.fori_loop(0, 8, spread_rows, 0)
+    pl.semaphore_wait(barrier, 5 - jnp.where(ty == 0, 1, 0) - jnp.where(ty == TILE_ROWS - 1, 1, 0))
     to_east = remote(edge, from_west, halo_send.at[0], halo_recv.at[0], east)
     to_west = remote(edge, from_east, halo_send.at[1], halo_recv.at[1], west)
     to_south = remote(s0.at[pl.ds(128, 3)], s0.at[pl.ds(0, 3)], halo_send.at[2], halo_recv.at[2], south)
     to_north = remote(s0.at[pl.ds(3, 3)], s0.at[pl.ds(131, 3)], halo_send.at[3], halo_recv.at[3], north)
-    to_east.start()
-    to_west.start()
+
+    @pl.when(ty < TILE_ROWS - 1)
+    def _():
+        to_east.start()
+
+    @pl.when(ty > 0)
+    def _():
+        to_west.start()
+
     to_south.start()
     to_north.start()
 
@@ -167,8 +186,16 @@
 
     out_west = cell < jnp.where(ty == 0, 4, 0)
     out_east = cell >= jnp.where(ty == TILE_ROWS - 1, 4, 8)
-    to_east.wait()
-    to_west.wait()
+    @pl.when(ty < TILE_ROWS - 1)
+    def _():
+        to_east.wait_send()
+        to_west.wait_recv()
+
+    @pl.when(ty > 0)
+    def _():
+        to_west.wait_send()
+        to_east.wait_recv()
+
     for strip in range(8):
         here = edge[strip]
         side[strip + 1, 0] = jnp.where(out_west, 0.0, jnp.where(cell < 4, from_west[strip], here))
@@ -178,10 +205,51 @@
     side_south.start()
     side_north.start()
 
+    def sides(group, which):
+        now = [side[n, which] for n in group]
+        last = len(now) - 1
+        for sweep in range(2):
+            down8 = [pltpu.roll(v, 8, 1) for v in now]
+            up8 = [pltpu.roll(v, 120, 1) for v in now]
+            later = []
+            for n, cur in enumerate(now):
+                upper = jnp.where(lane < 8, down8[max(n - 1, 0)], down8[n])
+                lower = jnp.where(lane >= 120, up8[min(n + 1, last)], up8[n])
+                value = substep(cur, upper, lower, pltpu.roll(cur, 1, 1), pltpu.roll(cur, 127, 1))
+                later.append(jnp.where(out_east if which else out_west, 0.0, value))
+            now = later
+        return now
+
+    def edge_values(group):
+        return [
+            jnp.where(
+                cell < 4, e, jnp.where(cell < 6, w, jnp.where(cell == 6, pltpu.roll(e, 2, 1), pltpu.roll(w, 4, 1)))
+            )
+            for w, e in zip(sides(group, 0), sides(group, 1), strict=True)
+        ]
+
+    def keep_edges(k):
+        shift = (0 if k in (1, 2) else 1 if k == 3 else -1)
+        at = 4 * sent + 1 + shift * d_sent
+        value = jnp.concatenate([strips[at + q] for q in (3, 2, 1, 0)], axis=0)
+        z_sent[k] = value
+        z_packs[k] = value.astype(BF16)
+        at = 4 * own + 1 + shift * d_own
+        z_own[k] = jnp.concatenate([strips[at + q] for q in range(4)], axis=0)
+
+    def z_copy(n):
+        return remote(z_packs.at[pl.ds(2 * n, 2)], z_arrived.at[pl.ds(2 * n, 2)], z_ssem.at[n], z_rsem.at[n], partner)
+
+    for n, value in enumerate(edge_values(range(1, 9))):
+        strips[n + 1] = value
+    keep_edges(0)
+    keep_edges(1)
+    z_copy(0).start()
+
     first_rows(3 + 1 + 61 * own)
     lax.fori_loop(0, 7, keep_packs, 0)
 
-    for load in loads[1:]:
+    for load in loads:
         load.wait()
     source = lax.broadcasted_iota(jnp.int32, (360, KIN), 0)
     for strip in range(STRIPS):
@@ -204,7 +272,7 @@
                 (c >= 0) & (c < CH) & (chan_out == c + CH * owner), 1.0, 0.0
             ).astype(BF16)
             w3[PACK * part : PACK * (part + 1), 256 * strip : 256 * (strip + 1)] = lax.dot_general(
-                pick, v_out[...], (((1,), (1,)), ((), ())), preferred_element_type=F32
+                pick, v_out[...], (((1,), (0,)), ((), ())), preferred_element_type=F32
             ).astype(BF16)
 
     to_south.wait()
@@ -212,40 +280,19 @@
     for index in (1, 2, 3, 130, 131, 132):
         s1[index] = advance_row(s0, index)
     lax.fori_loop(7, 9, send_packs, 0)
+    lax.fori_loop(7, 9, keep_packs, 0)
 
     side_south.wait()
     side_north.wait()
-    now = [[side[n, which] for n in range(10)] for which in range(2)]
-    for sweep in range(2):
-        later = []
-        for which in range(2):
-            cur = now[which]
-            down8 = [pltpu.roll(v, 8, 1) for v in cur]
-            up8 = [pltpu.roll(v, 120, 1) for v in cur]
-            new = []
-            for n in range(10):
-                upper = jnp.where(lane < 8, down8[max(n - 1, 0)], down8[n])
-                lower = jnp.where(lane >= 120, up8[min(n + 1, 9)], up8[n])
-                value = substep(cur[n], upper, lower, pltpu.roll(cur[n], 1, 1), pltpu.roll(cur[n], 127, 1))
-                new.append(jnp.where(out_east if which else out_west, 0.0, value))
-            later.append(new)
-        now = later
-    for n in range(10):
-        w, e = now[0][n], now[1][n]
-        strips[n] = jnp.where(
-            cell < 4, e, jnp.where(cell < 6, w, jnp.where(cell == 6, pltpu.roll(e, 2, 1), pltpu.roll(w, 4, 1)))
-        )
-    for k in range(3):
-        at = 4 * sent + 1 + (k - 1) * d_sent
-        value = jnp.concatenate([strips[at + q] for q in (3, 2, 1, 0)], axis=0)
-        z_sent[k] = value
-        z_packs[k] = value.astype(BF16)
-    z_copy = remote(z_packs, z_arrived, z_sem.at[0], z_sem.at[1], partner)
-    z_copy.start()
-    for k in range(3):
-        at = 4 * own + 1 + (k - 1) * d_own
-        z_own[k] = jnp.concatenate([strips[at + q] for q in range(4)], axis=0)
-    lax.fori_loop(7, 9, keep_packs, 0)
+    first, second = edge_values((0, 1))
+    strips[0] = first
+    strips[1] = jnp.where(lane < 16, second, strips[1])
+    second, last = edge_values((8, 9))
+    strips[8] = jnp.where(lane >= 112, second, strips[8])
+    strips[9] = last
+    keep_edges(2)
+    keep_edges(3)
+    z_copy(1).start()
 
     lane1 = lax.broadcasted_iota(jnp.int32, (1, 128), 1)
 
@@ -275,7 +322,7 @@
 
     def ingest(slot):
         place = lax.rem(15 * (1 - own) + d_own * (slot - 1) + 16, 16)
-        zi = (slot + 16) // 17 + slot // 17
+        zi = (slot + 16) // 17 + slot // 15 + slot // 17
         for which in range(2):
             if which == 0:
                 value, z = moved_own[slot], z_own[zi]
@@ -291,7 +338,7 @@
 
     sub = lax.broadcasted_iota(jnp.int32, (16, 128), 0)
 
-    def pick_neighbours(slot, u):
+    def pick_neighbours(slot, u, xs):
         cols = slice(128 * u, 128 * (u + 1))
         tails = {}
         for which in range(2):
@@ -330,68 +377,85 @@
         for p, q in enumerate(order):
             flat_out[pl.ds(64 * half + 16 * q + place, CH, stride=128), :] = value[CH * p : CH * (p + 1)]
 
-    flat_out = result.reshape(CH * 128, 128)
+    flat_out = out.reshape(CH * 128, 128)
 
     def t_copy(t):
         return remote(t_send.at[t], t_arrived.at[t], t_ssem.at[t], t_rsem.at[t], partner)
 
-    z_copy.wait()
-    pack_copy(0).wait_recv()
-    ingest(0)
-    ingest(1)
-
-    def physics(t, carry):
-        pack_copy(t + 1).wait_recv()
-        ingest(2 * t + 2)
-        ingest(2 * t + 3)
-        for u in range(2):
-            pick_neighbours(2 * t + 1 + u, u)
+    def network(t, xs):
+        halves = [jnp.dot(w1[q], xs[q], preferred_element_type=F32) for q in range(STRIPS)]
+        first = [silu_of_double(h).astype(BF16) for h in halves]
+        halves = [jnp.dot(w2[...], h, preferred_element_type=F32) for h in first]
         for q in range(STRIPS):
-            first = silu_of_double(jnp.dot(w1[q], xs[q], preferred_element_type=F32)).astype(BF16)
-            second = silu_of_double(jnp.dot(w2[...], first, preferred_element_type=F32)).astype(BF16)
-            ys[256 * q : 256 * (q + 1), :] = second
+            ys[256 * q : 256 * (q + 1), :] = silu_of_double(halves[q]).astype(BF16)
         tendency = jnp.dot(w3[...], ys[...], preferred_element_type=F32).astype(BF16)
         for u in range(2):
             t_send[t, u] = tendency[PACK:, 128 * u : 128 * (u + 1)]
-        t_copy(t).start()
         for u in range(2):
             place = 15 * (1 - own) + d_own * (2 * t + u)
             value = moved_own[2 * t + 1 + u] + tendency[:PACK, 128 * u : 128 * (u + 1)].astype(F32)
             store_rows(value, own, place, (0, 1, 2, 3))
+
+    z_copy(0).wait_recv()
+    pack_copy(0).wait_recv()
+    pack_copy(1).wait_recv()
+    for slot in range(4):
+        ingest(slot)
+    for u in range(2):
+        pick_neighbours(1 + u, u, xs_even)
+
+    def physics(p, carry):
+        for odd, (here, there) in enumerate(((xs_even, xs_odd), (xs_odd, xs_even))):
+            t = 2 * p + odd
+
+            @pl.when(t < STEPS - 1)
+            def _():
+                pack_copy(t + 2).wait_recv()
+
+            @pl.when(t == 5)
+            def _():
+                z_copy(1).wait_recv()
+
+            ahead = jnp.minimum(t, STEPS - 2)
+            ingest(2 * ahead + 4)
+            ingest(2 * ahead + 5)
+            for u in range(2):
+                pick_neighbours(2 * ahead + 3 + u, u, there)
+            network(t, here)
+            t_copy(t).start()
         return carry
 
-    lax.fori_loop(0, STEPS, physics, 0)
+    lax.fori_loop(0, STEPS // 2, physics, 0)
 
     def finish(t, carry):
         t_copy(t).wait_recv()
         for u in range(2):
             place = 15 * (1 - sent) + d_sent * (2 * t + u)
-            value = fix_edges(moved_sent[2 * t + 1 + u], z_sent[1], place) + t_arrived[t, u].astype(F32)
+            value = fix_edges(moved_sent[2 * t + 1 + u], z_sent[2], place) + t_arrived[t, u].astype(F32)
             store_rows(value, sent, place, (3, 2, 1, 0))
         return carry
 
     lax.fori_loop(0, STEPS, finish, 0)
-    store = pltpu.make_async_copy(result, out, out_sem)
-    store.start()
+    z_copy(0).wait_send()
+    z_copy(1).wait_send()
     for s in range(SENDS):
         pack_copy(s).wait_send()
     for t in range(STEPS):
         t_copy(t).wait_send()
-    store.wait()
 
 
 def shards(state, courant_x, courant_y, diffusion, neighbours, w_in, w_mid, w_out):
     levels, fields, single, cells_x, cells_y = state.shape
     chans = levels * fields
-    anywhere = pl.BlockSpec(memory_space=pl.ANY)
+    anywhere = pl.BlockSpec(memory_space=pltpu.HBM)
     scalars = pl.BlockSpec(memory_space=pltpu.SMEM)
     vmem = pltpu.VMEM
     dma = pltpu.SemaphoreType.DMA
     updated = pl.pallas_call(
         kernel,
-        out_shape=jax.ShapeDtypeStruct((chans, cells_x, cells_y), F32),
+        out_shape=pltpu.VMEM((chans, cells_x, cells_y), F32),
         in_specs=[anywhere, scalars, scalars, scalars, anywhere, anywhere, anywhere, anywhere, anywhere],
-        out_specs=anywhere,
+        out_specs=pl.BlockSpec(memory_space=vmem),
         scratch_shapes=[
             vmem((CH, 128, 128), F32),
             vmem((134, CH, 128), F32),
@@ -406,17 +470,18 @@
             vmem((SLOTS, PACK, 128), F32),
             vmem((SLOTS, PACK, 128), BF16),
             vmem((SLOTS, PACK, 128), BF16),
-            vmem((3, PACK, 128), F32),
-            vmem((3, PACK, 128), F32),
-            vmem((3, PACK, 128), BF16),
-            vmem((3, PACK, 128), BF16),
+            vmem((4, PACK, 128), F32),
+            vmem((4, PACK, 128), F32),
+            vmem((4, PACK, 128), BF16),
+            vmem((4, PACK, 128), BF16),
             vmem((2, SLOTS, 3, PACK, 128), BF16),
             vmem((2, 16, 3, PACK, 128), BF16),
+            vmem((STRIPS, KIN, 256), BF16),
             vmem((STRIPS, KIN, 256), BF16),
             vmem((STRIPS * 256, 256), BF16),
             vmem((360, 256), BF16),
             vmem((256, 256), BF16),
-            vmem((256, 40), BF16),
+            vmem((40, 256), BF16),
             vmem((STRIPS, 256, KIN), BF16),
             vmem((256, 256), BF16),
             vmem((2 * PACK, STRIPS * 256), BF16),
@@ -424,19 +489,19 @@
             vmem((STRIPS, 1, KIN), jnp.int32),
             vmem((STEPS, 2, PACK, 128), BF16),
             vmem((STEPS, 2, PACK, 128), BF16),
-            vmem((CH, 128, 128), F32),
+            dma((8,)),
             dma((6,)),
             dma((SENDS,)),
             dma((SENDS,)),
+            dma((2,)),
             dma((2,)),
             dma((STEPS,)),
             dma((STEPS,)),
             dma((6,)),
             dma((6,)),
-            dma,
         ],
         compiler_params=pltpu.CompilerParams(
-            collective_id=0, has_side_effects=True, vmem_limit_bytes=48 * 1024 * 1024
+            collective_id=0, has_side_effects=True, vmem_limit_bytes=60900 * 1024
         ),
     )(
         state.reshape(chans, cells_x, cells_y),
@@ -446,7 +511,7 @@
         neighbours.reshape(9, cells_x, cells_y),
         w_in,
         w_mid,
-        w_out,
+        w_out.T,
         jnp.asarray(feature_rows()),
     )
     return updated.reshape(levels, fields, single, cells_x, cells_y)

time: 54.1 us -> 35.1 us (0.65)
  Pallas kernels: 45 us -> 34 us
  local copies, waits for them, and re-layouts: 8.79 us -> 1.06 us
    pallas_call x1, Pallas kernels: 45 us -> 34 us  [shards(): pl.pallas_call(kernel, out_shape=pltpu.VMEM((chans, cells_x, cells_y), F3...]
    unnamed x18 -> x1, local copies, waits for them, and re-layouts: 8.79 us -> 1.06 us
where the time goes in v1:
time: 35.1 us; the launch traced here: 35 us
  Pallas kernels  34 us (97%)
  local copies, waits for them, and re-layouts  1.06 us (3%)
    pallas_call x1, Pallas kernels, shards(): pl.pallas_call(kernel, out_shape=pltpu.VMEM((chans, cells_x, cells_y), F3...  34 us
    unnamed x1, local copies, waits for them, and re-layouts  1.06 us

profile of v1, /device:TPU:1, one launch (start us, length us, event | category | flops | bytes accessed | tf_op | source)
XLA Modules:
  0.0 35.0 jit_solution(8939540759666630781)
XLA Ops:
  0.0 34.0 %shard_map.91 = f32[20,128,128]{2,1,0:T(8,128)S(1)} custom-call(f32[20,128,128]{2,1,0:T(8,128)} %bitcast.7, f32[4]{0:T(128)} %speed_x.1, f32[4]{0:T(128)} %speed_y.1, f32[5]{0:T(128)} %spread.1, s32[9,128,128]{2,1,0:T(8,128)} %bitcast.8, bf16[360,256]{1,0:T(8,128)(2,1)} %w_in.1, bf16[256,256]{1,0:T(8,128)(2,1)} %w_mid.1, bf16[40,256]{1,0:T(8,128)(2,1)} %bitcast.9, ...), custom_call_target="tpu_custom_call" | custom-call | tf_op jit(solution)/shard_map/pallas_call | solution.py:454
  34.0 1.1 %copy.12 = f32[4,5,1,128,128]{4,3,2,1,0:T(8,128)} copy(f32[4,5,1,128,128]{4,3,2,1,0:T(8,128)S(1)} %bitcast.6) | data formatting | bytes 2621440

commit v2 on v1

--- a/solution.py
+++ b/solution.py
@@ -15,6 +15,7 @@
 SLOTS = 18
 SENDS = SLOTS // 2
 STEPS = 8
+AHEAD = 3
 KIN = 9 * 48
 
 
@@ -38,7 +39,7 @@
 
 def kernel(
     state, speed_x, speed_y, spread, near, w_in, w_mid, w_out, table, out,
-    xv, s0, s1, coef, edge, from_west, from_east, side, strips, moved_own, moved_sent, packs, arrived,
+    xv, s0, s1, coef, edge, edge_out, from_west, from_east, side, strips, moved_own, moved_sent, packs, arrived,
     z_own, z_sent, z_packs, z_arrived, shifted, masks, xs_even, xs_odd, ys, v_in, v_mid, v_out, w1, w2, w3, nb, tv,
     t_send, t_arrived,
     state_sem, load_sem, pack_send, pack_recv, z_ssem, z_rsem, t_ssem, t_rsem, halo_send, halo_recv,
@@ -73,10 +74,10 @@
         rows = pl.ds(pl.multiple_of(16 * n, 16), 16)
         return pltpu.make_async_copy(state.at[:, rows], xv.at[:, rows], state_sem.at[n])
 
+    for load in loads:
+        load.start()
     for n in range(8):
         state_load(n).start()
-    for load in loads:
-        load.start()
     barrier = pltpu.get_barrier_semaphore()
     for device in (north, south, partner):
         pl.semaphore_signal(barrier, inc=1, device_id=device, device_id_type=MESH)
@@ -118,6 +119,28 @@
             center, src[index - 1], src[index + 1], pltpu.roll(center, 1, 1), pltpu.roll(center, 127, 1)
         )
 
+    loads[3].wait()
+    lane1 = lax.broadcasted_iota(jnp.int32, (1, 128), 1)
+
+    def order_masks(m, carry):
+        place = 15 * (1 - own) + d_own * m
+        flips = [[], [], []]
+        for q in range(STRIPS):
+            row = 16 * q + place
+            centre = (64 * g + row + 1) * 130 + lane1 + 1
+            first = nb[0, pl.ds(row, 1), :] - centre
+            second = nb[1, pl.ds(row, 1), :] - centre
+            flips[0].append(jnp.where(first > 0, 1.0, 0.0))
+            flips[1].append(jnp.where((first == -129) | (first == 131), 1.0, 0.0))
+            flips[2].append(jnp.where(second * second == 1, 1.0, 0.0))
+        for kind in range(3):
+            wide = [jnp.broadcast_to(v, (CH, 128)) for v in flips[kind]]
+            masks[0, m, kind] = jnp.concatenate(wide, axis=0).astype(BF16)
+            masks[1, m, kind] = jnp.concatenate(wide[::-1], axis=0).astype(BF16)
+        return carry
+
+    lax.fori_loop(0, 16, order_masks, 0)
+
     flat = xv.reshape(CH * 128, 128)
 
     def spread_rows(strip, carry):
@@ -131,9 +154,12 @@
         return carry
 
     lax.fori_loop(0, 8, spread_rows, 0)
+    for n in range(4):
+        edge_out[0, n] = jnp.where(cell < 4, edge[n], pltpu.roll(edge[n + 4], 4, 1))
+        edge_out[1, n] = jnp.where(cell < 4, pltpu.roll(edge[n + 4], 124, 1), edge[n])
     pl.semaphore_wait(barrier, 5 - jnp.where(ty == 0, 1, 0) - jnp.where(ty == TILE_ROWS - 1, 1, 0))
-    to_east = remote(edge, from_west, halo_send.at[0], halo_recv.at[0], east)
-    to_west = remote(edge, from_east, halo_send.at[1], halo_recv.at[1], west)
+    to_east = remote(edge_out.at[0], from_west, halo_send.at[0], halo_recv.at[0], east)
+    to_west = remote(edge_out.at[1], from_east, halo_send.at[1], halo_recv.at[1], west)
     to_south = remote(s0.at[pl.ds(128, 3)], s0.at[pl.ds(0, 3)], halo_send.at[2], halo_recv.at[2], south)
     to_north = remote(s0.at[pl.ds(3, 3)], s0.at[pl.ds(131, 3)], halo_send.at[3], halo_recv.at[3], north)
 
@@ -182,74 +208,10 @@
         return carry
 
     first_rows(3 + 1 + 61 * sent)
-    lax.fori_loop(0, 7, send_packs, 0)
-
-    out_west = cell < jnp.where(ty == 0, 4, 0)
-    out_east = cell >= jnp.where(ty == TILE_ROWS - 1, 4, 8)
-    @pl.when(ty < TILE_ROWS - 1)
-    def _():
-        to_east.wait_send()
-        to_west.wait_recv()
-
-    @pl.when(ty > 0)
-    def _():
-        to_west.wait_send()
-        to_east.wait_recv()
-
-    for strip in range(8):
-        here = edge[strip]
-        side[strip + 1, 0] = jnp.where(out_west, 0.0, jnp.where(cell < 4, from_west[strip], here))
-        side[strip + 1, 1] = jnp.where(out_east, 0.0, jnp.where(cell < 4, here, from_east[strip]))
-    side_south = remote(side.at[8], side.at[0], halo_send.at[4], halo_recv.at[4], south)
-    side_north = remote(side.at[1], side.at[9], halo_send.at[5], halo_recv.at[5], north)
-    side_south.start()
-    side_north.start()
-
-    def sides(group, which):
-        now = [side[n, which] for n in group]
-        last = len(now) - 1
-        for sweep in range(2):
-            down8 = [pltpu.roll(v, 8, 1) for v in now]
-            up8 = [pltpu.roll(v, 120, 1) for v in now]
-            later = []
-            for n, cur in enumerate(now):
-                upper = jnp.where(lane < 8, down8[max(n - 1, 0)], down8[n])
-                lower = jnp.where(lane >= 120, up8[min(n + 1, last)], up8[n])
-                value = substep(cur, upper, lower, pltpu.roll(cur, 1, 1), pltpu.roll(cur, 127, 1))
-                later.append(jnp.where(out_east if which else out_west, 0.0, value))
-            now = later
-        return now
-
-    def edge_values(group):
-        return [
-            jnp.where(
-                cell < 4, e, jnp.where(cell < 6, w, jnp.where(cell == 6, pltpu.roll(e, 2, 1), pltpu.roll(w, 4, 1)))
-            )
-            for w, e in zip(sides(group, 0), sides(group, 1), strict=True)
-        ]
-
-    def keep_edges(k):
-        shift = (0 if k in (1, 2) else 1 if k == 3 else -1)
-        at = 4 * sent + 1 + shift * d_sent
-        value = jnp.concatenate([strips[at + q] for q in (3, 2, 1, 0)], axis=0)
-        z_sent[k] = value
-        z_packs[k] = value.astype(BF16)
-        at = 4 * own + 1 + shift * d_own
-        z_own[k] = jnp.concatenate([strips[at + q] for q in range(4)], axis=0)
-
-    def z_copy(n):
-        return remote(z_packs.at[pl.ds(2 * n, 2)], z_arrived.at[pl.ds(2 * n, 2)], z_ssem.at[n], z_rsem.at[n], partner)
-
-    for n, value in enumerate(edge_values(range(1, 9))):
-        strips[n + 1] = value
-    keep_edges(0)
-    keep_edges(1)
-    z_copy(0).start()
-
+    lax.fori_loop(0, AHEAD, send_packs, 0)
     first_rows(3 + 1 + 61 * own)
-    lax.fori_loop(0, 7, keep_packs, 0)
-
-    for load in loads:
+
+    for load in loads[:3] + loads[4:]:
         load.wait()
     source = lax.broadcasted_iota(jnp.int32, (360, KIN), 0)
     for strip in range(STRIPS):
@@ -275,45 +237,74 @@
                 pick, v_out[...], (((1,), (0,)), ((), ())), preferred_element_type=F32
             ).astype(BF16)
 
-    to_south.wait()
-    to_north.wait()
-    for index in (1, 2, 3, 130, 131, 132):
-        s1[index] = advance_row(s0, index)
-    lax.fori_loop(7, 9, send_packs, 0)
-    lax.fori_loop(7, 9, keep_packs, 0)
-
-    side_south.wait()
-    side_north.wait()
-    first, second = edge_values((0, 1))
-    strips[0] = first
-    strips[1] = jnp.where(lane < 16, second, strips[1])
-    second, last = edge_values((8, 9))
-    strips[8] = jnp.where(lane >= 112, second, strips[8])
-    strips[9] = last
-    keep_edges(2)
-    keep_edges(3)
-    z_copy(1).start()
-
-    lane1 = lax.broadcasted_iota(jnp.int32, (1, 128), 1)
-
-    def order_masks(m, carry):
-        place = 15 * (1 - own) + d_own * m
-        flips = [[], [], []]
-        for q in range(STRIPS):
-            row = 16 * q + place
-            centre = (64 * g + row + 1) * 130 + lane1 + 1
-            first = nb[0, pl.ds(row, 1), :] - centre
-            second = nb[1, pl.ds(row, 1), :] - centre
-            flips[0].append(jnp.where(first > 0, 1.0, 0.0))
-            flips[1].append(jnp.where((first == -129) | (first == 131), 1.0, 0.0))
-            flips[2].append(jnp.where(second * second == 1, 1.0, 0.0))
-        for kind in range(3):
-            wide = [jnp.broadcast_to(v, (CH, 128)) for v in flips[kind]]
-            masks[0, m, kind] = jnp.concatenate(wide, axis=0).astype(BF16)
-            masks[1, m, kind] = jnp.concatenate(wide[::-1], axis=0).astype(BF16)
-        return carry
-
-    lax.fori_loop(0, 16, order_masks, 0)
+
+    out_west = cell < jnp.where(ty == 0, 4, 0)
+    out_east = cell >= jnp.where(ty == TILE_ROWS - 1, 4, 8)
+    @pl.when(ty < TILE_ROWS - 1)
+    def _():
+        to_east.wait_send()
+        to_west.wait_recv()
+
+    @pl.when(ty > 0)
+    def _():
+        to_west.wait_send()
+        to_east.wait_recv()
+
+    for strip in range(8):
+        here = edge[strip]
+        beyond_west, beyond_east = from_west[strip % 4], from_east[strip % 4]
+        if strip >= 4:
+            beyond_west, beyond_east = pltpu.roll(beyond_west, 124, 1), pltpu.roll(beyond_east, 4, 1)
+        side[strip + 1, 0] = jnp.where(out_west, 0.0, jnp.where(cell < 4, beyond_west, here))
+        side[strip + 1, 1] = jnp.where(out_east, 0.0, jnp.where(cell < 4, here, beyond_east))
+    side_south = remote(side.at[8], side.at[0], halo_send.at[4], halo_recv.at[4], south)
+    side_north = remote(side.at[1], side.at[9], halo_send.at[5], halo_recv.at[5], north)
+    side_south.start()
+    side_north.start()
+
+    def sides(group, which):
+        now = [side[n, which] for n in group]
+        last = len(now) - 1
+        for sweep in range(2):
+            down8 = [pltpu.roll(v, 8, 1) for v in now]
+            up8 = [pltpu.roll(v, 120, 1) for v in now]
+            later = []
+            for n, cur in enumerate(now):
+                upper = jnp.where(lane < 8, down8[max(n - 1, 0)], down8[n])
+                lower = jnp.where(lane >= 120, up8[min(n + 1, last)], up8[n])
+                value = substep(cur, upper, lower, pltpu.roll(cur, 1, 1), pltpu.roll(cur, 127, 1))
+                later.append(jnp.where(out_east if which else out_west, 0.0, value))
+            now = later
+        return now
+
+    def edge_values(group):
+        return [
+            jnp.where(
+                cell < 4, e, jnp.where(cell < 6, w, jnp.where(cell == 6, pltpu.roll(e, 2, 1), pltpu.roll(w, 4, 1)))
+            )
+            for w, e in zip(sides(group, 0), sides(group, 1), strict=True)
+        ]
+
+    def keep_edges(k):
+        shift = (0 if k in (1, 2) else 1 if k == 3 else -1)
+        at = 4 * sent + 1 + shift * d_sent
+        value = jnp.concatenate([strips[at + q] for q in (3, 2, 1, 0)], axis=0)
+        z_sent[k] = value
+        z_packs[k] = value.astype(BF16)
+        at = 4 * own + 1 + shift * d_own
+        z_own[k] = jnp.concatenate([strips[at + q] for q in range(4)], axis=0)
+
+    def z_copy(n):
+        return remote(z_packs.at[pl.ds(2 * n, 2)], z_arrived.at[pl.ds(2 * n, 2)], z_ssem.at[n], z_rsem.at[n], partner)
+
+    for n, value in enumerate(edge_values(range(1, 9))):
+        strips[n + 1] = value
+    keep_edges(0)
+    keep_edges(1)
+    z_copy(0).start()
+
+    lax.fori_loop(AHEAD, 7, send_packs, 0)
+    lax.fori_loop(0, 2, keep_packs, 0)
 
     wide_lane = lax.broadcasted_iota(jnp.int32, (PACK, 128), 1)
 
@@ -382,10 +373,37 @@
     def t_copy(t):
         return remote(t_send.at[t], t_arrived.at[t], t_ssem.at[t], t_rsem.at[t], partner)
 
-    def network(t, xs):
-        halves = [jnp.dot(w1[q], xs[q], preferred_element_type=F32) for q in range(STRIPS)]
-        first = [silu_of_double(h).astype(BF16) for h in halves]
-        halves = [jnp.dot(w2[...], h, preferred_element_type=F32) for h in first]
+    def borders():
+        to_south.wait()
+        to_north.wait()
+        for index in (1, 2, 3, 130, 131, 132):
+            s1[index] = advance_row(s0, index)
+        lax.fori_loop(7, 9, send_packs, 0)
+
+        side_south.wait()
+        side_north.wait()
+        first, second = edge_values((0, 1))
+        strips[0] = first
+        strips[1] = jnp.where(lane < 16, second, strips[1])
+        second, last = edge_values((8, 9))
+        strips[8] = jnp.where(lane >= 112, second, strips[8])
+        strips[9] = last
+        keep_edges(2)
+        keep_edges(3)
+        z_copy(1).start()
+
+    def network(t, xs, beside):
+        halves, first = [], []
+        for q in range(STRIPS):
+            halves.append(jnp.dot(w1[q], xs[q], preferred_element_type=F32))
+            if q == 1:
+                beside[0]()
+        for q in range(STRIPS):
+            first.append(silu_of_double(halves[q]).astype(BF16))
+            halves[q] = jnp.dot(w2[...], first[q], preferred_element_type=F32)
+            if q == 1:
+                beside[1]()
+        beside[2]()
         for q in range(STRIPS):
             ys[256 * q : 256 * (q + 1), :] = silu_of_double(halves[q]).astype(BF16)
         tendency = jnp.dot(w3[...], ys[...], preferred_element_type=F32).astype(BF16)
@@ -404,28 +422,44 @@
     for u in range(2):
         pick_neighbours(1 + u, u, xs_even)
 
+    nothing = (lambda: None,) * 3
+
+    def beside(t, xs):
+        def prepare():
+            keep_packs(t + 2, 0)
+            ingest(2 * t + 4)
+            ingest(2 * t + 5)
+
+        return (
+            prepare,
+            lambda: pick_neighbours(2 * t + 3, 0, xs),
+            lambda: pick_neighbours(2 * t + 4, 1, xs),
+        )
+
     def physics(p, carry):
         for odd, (here, there) in enumerate(((xs_even, xs_odd), (xs_odd, xs_even))):
             t = 2 * p + odd
-
-            @pl.when(t < STEPS - 1)
-            def _():
-                pack_copy(t + 2).wait_recv()
-
-            @pl.when(t == 5)
-            def _():
-                z_copy(1).wait_recv()
-
-            ahead = jnp.minimum(t, STEPS - 2)
-            ingest(2 * ahead + 4)
-            ingest(2 * ahead + 5)
-            for u in range(2):
-                pick_neighbours(2 * ahead + 3 + u, u, there)
-            network(t, here)
+            pack_copy(t + 2).wait_recv()
+            if odd:
+
+                @pl.when(p == 0)
+                def _():
+                    borders()
+
+                @pl.when(p == 2)
+                def _():
+                    z_copy(1).wait_recv()
+
+            network(t, here, beside(t, there))
             t_copy(t).start()
         return carry
 
-    lax.fori_loop(0, STEPS // 2, physics, 0)
+    lax.fori_loop(0, STEPS // 2 - 1, physics, 0)
+    pack_copy(STEPS).wait_recv()
+    network(STEPS - 2, xs_even, beside(STEPS - 2, xs_odd))
+    t_copy(STEPS - 2).start()
+    network(STEPS - 1, xs_odd, nothing)
+    t_copy(STEPS - 1).start()
 
     def finish(t, carry):
         t_copy(t).wait_recv()
@@ -462,8 +496,9 @@
             vmem((134, CH, 128), F32),
             vmem((5, CH, 128), F32),
             vmem((8, CH, 128), F32),
-            vmem((8, CH, 128), F32),
-            vmem((8, CH, 128), F32),
+            vmem((2, 4, CH, 128), F32),
+            vmem((4, CH, 128), F32),
+            vmem((4, CH, 128), F32),
             vmem((10, 2, CH, 128), F32),
             vmem((10, CH, 128), F32),
             vmem((SLOTS, PACK, 128), F32),

time: 35.1 us -> 32.8 us (0.934)
  Pallas kernels: 34 us -> 31.5 us
    pallas_call x1, Pallas kernels: 34 us -> 31.5 us  [shards(): pl.pallas_call(kernel, out_shape=pltpu.VMEM((chans, cells_x, cells_y), F3...]
where the time goes in v2:
time: 32.8 us; the launch traced here: 32.6 us
  Pallas kernels  31.5 us (96%)
  local copies, waits for them, and re-layouts  1.06 us (3%)
    pallas_call x1, Pallas kernels, shards(): pl.pallas_call(kernel, out_shape=pltpu.VMEM((chans, cells_x, cells_y), F3...  31.5 us
    unnamed x1, local copies, waits for them, and re-layouts  1.06 us

profile of v2, /device:TPU:1, one launch (start us, length us, event | category | flops | bytes accessed | tf_op | source)
XLA Modules:
  0.0 32.6 jit_solution(12502861529461360065)
XLA Ops:
  0.0 31.5 %shard_map.91 = f32[20,128,128]{2,1,0:T(8,128)S(1)} custom-call(f32[20,128,128]{2,1,0:T(8,128)} %bitcast.7, f32[4]{0:T(128)} %speed_x.1, f32[4]{0:T(128)} %speed_y.1, f32[5]{0:T(128)} %spread.1, s32[9,128,128]{2,1,0:T(8,128)} %bitcast.8, bf16[360,256]{1,0:T(8,128)(2,1)} %w_in.1, bf16[256,256]{1,0:T(8,128)(2,1)} %w_mid.1, bf16[40,256]{1,0:T(8,128)(2,1)} %bitcast.9, ...), custom_call_target="tpu_custom_call" | custom-call | tf_op jit(solution)/shard_map/pallas_call | solution.py:488
  31.5 1.1 %copy.12 = f32[4,5,1,128,128]{4,3,2,1,0:T(8,128)} copy(f32[4,5,1,128,128]{4,3,2,1,0:T(8,128)S(1)} %bitcast.6) | data formatting | bytes 2621440

commit v3 on v2

--- a/solution.py
+++ b/solution.py
@@ -74,8 +74,7 @@
         rows = pl.ds(pl.multiple_of(16 * n, 16), 16)
         return pltpu.make_async_copy(state.at[:, rows], xv.at[:, rows], state_sem.at[n])
 
-    for load in loads:
-        load.start()
+    loads[3].start()
     for n in range(8):
         state_load(n).start()
     barrier = pltpu.get_barrier_semaphore()
@@ -89,6 +88,9 @@
     @pl.when(ty < TILE_ROWS - 1)
     def _():
         pl.semaphore_signal(barrier, inc=1, device_id=east, device_id_type=MESH)
+
+    for load in loads[:3] + loads[4:]:
+        load.start()
 
     chan = lax.broadcasted_iota(jnp.int32, (CH, 128), 0)
     ax = jnp.zeros((CH, 128), F32)
@@ -409,6 +411,7 @@
         tendency = jnp.dot(w3[...], ys[...], preferred_element_type=F32).astype(BF16)
         for u in range(2):
             t_send[t, u] = tendency[PACK:, 128 * u : 128 * (u + 1)]
+        t_copy(t).start()
         for u in range(2):
             place = 15 * (1 - own) + d_own * (2 * t + u)
             value = moved_own[2 * t + 1 + u] + tendency[:PACK, 128 * u : 128 * (u + 1)].astype(F32)
@@ -451,15 +454,12 @@
                     z_copy(1).wait_recv()
 
             network(t, here, beside(t, there))
-            t_copy(t).start()
         return carry
 
     lax.fori_loop(0, STEPS // 2 - 1, physics, 0)
     pack_copy(STEPS).wait_recv()
     network(STEPS - 2, xs_even, beside(STEPS - 2, xs_odd))
-    t_copy(STEPS - 2).start()
     network(STEPS - 1, xs_odd, nothing)
-    t_copy(STEPS - 1).start()
 
     def finish(t, carry):
         t_copy(t).wait_recv()

time: 32.8 us -> 33.4 us (1.018)
  Pallas kernels: 31.5 us -> 32.2 us
    pallas_call x1, Pallas kernels: 31.5 us -> 32.2 us  [shards(): pl.pallas_call(kernel, out_shape=pltpu.VMEM((chans, cells_x, cells_y), F3...]
where the time goes in v3:
time: 33.4 us; the launch traced here: 33.3 us
  Pallas kernels  32.2 us (96%)
  local copies, waits for them, and re-layouts  1.06 us (3%)
    pallas_call x1, Pallas kernels, shards(): pl.pallas_call(kernel, out_shape=pltpu.VMEM((chans, cells_x, cells_y), F3...  32.2 us
    unnamed x1, local copies, waits for them, and re-layouts  1.06 us

profile of v3, /device:TPU:1, one launch (start us, length us, event | category | flops | bytes accessed | tf_op | source)
XLA Modules:
  0.0 33.3 jit_solution(5117712082340169224)
XLA Ops:
  0.0 32.2 %shard_map.91 = f32[20,128,128]{2,1,0:T(8,128)S(1)} custom-call(f32[20,128,128]{2,1,0:T(8,128)} %bitcast.7, f32[4]{0:T(128)} %speed_x.1, f32[4]{0:T(128)} %speed_y.1, f32[5]{0:T(128)} %spread.1, s32[9,128,128]{2,1,0:T(8,128)} %bitcast.8, bf16[360,256]{1,0:T(8,128)(2,1)} %w_in.1, bf16[256,256]{1,0:T(8,128)(2,1)} %w_mid.1, bf16[40,256]{1,0:T(8,128)(2,1)} %bitcast.9, ...), custom_call_target="tpu_custom_call" | custom-call | tf_op jit(solution)/shard_map/pallas_call | solution.py:488
  32.2 1.1 %copy.12 = f32[4,5,1,128,128]{4,3,2,1,0:T(8,128)} copy(f32[4,5,1,128,128]{4,3,2,1,0:T(8,128)S(1)} %bitcast.6) | data formatting | bytes 2621440
